TPU v7x, 32 devices: a whole 2x2x4 slice. The times are simulated.
32 devices in a mesh: dp: 4 (over z), seq: 8 (over y, x, core).
Axes of the slice: x: 2, y: 2, z: 4, core: 2. Of those that a mesh axis runs over, the one named last changes fastest.
Arguments:
- queries: bfloat16 [4096, 4096], P(('dp', 'seq')), may hold values from -6 to 6
- keys: bfloat16 [4096, 512], P(('dp', 'seq')), may hold values from -6 to 6
- values: bfloat16 [4096, 512], P(('dp', 'seq')), may hold values from -6 to 6
- grad_out: bfloat16 [4096, 4096], P(('dp', 'seq')), may hold values from -6 to 6
- doc_lengths: int32 [16], replicated, may hold values from 1 to 1024, 4096 in all
Outputs:
- grad_q: bfloat16 [4096, 4096], P(('dp', 'seq'))
- grad_k: bfloat16 [4096, 512], P(('dp', 'seq'))
- grad_v: bfloat16 [4096, 512], P(('dp', 'seq'))
Inputs may be any that keep to these rules, and one draw needn't show every extreme that they name: `doc_lengths`: the 16 lengths sum to 4096; the longest is exactly 1024.
All inputs are finite; a program needn't handle non-finite values.
Results may differ from a plain program's by a relative error of at most 0.0071.
Values may be sent and summed in bfloat16 or wider, within the bound.
No kernel may reach another device: no remote copies, remote signals or barrier semaphores. Data moves between devices by JAX's collectives and lax.ppermute only.
A program may use at most 64 MiB of HBM per device.

v0:
```python
import functools

import jax
import jax.numpy as jnp
from jax import lax
from jax.experimental import pallas as pl
from jax.experimental.pallas import tpu as pltpu
from jax.sharding import PartitionSpec as P

QH = 32
KVH = 4
HD = 128
PER_KV = QH // KVH
GROUPS = KVH // 2
MIB = 1024 * 1024
INV_ROOT = HD ** -0.5
TO_LOG2 = INV_ROOT * 1.4426950408889634
NT = (((1,), (1,)), ((), ()))
NN = (((1,), (0,)), ((), ()))
TN = (((0,), (0,)), ((), ()))
K_COLS = pl.ds(0, HD)
V_COLS = pl.ds(HD, HD)


def dot(a, b, dims):
    return lax.dot_general(a, b, dims, preferred_element_type=jnp.float32)


def distance(pair, k, pairs):
    return lax.rem(pair - (pair ^ k) + pairs, pairs)


def place(info_ref, doc_ref, tok, pairs):
    core = lax.rem(info_ref[1], 2)
    chip = info_ref[0] * pairs + info_ref[1] // 2
    first = chip * 2 * tok
    pos = [
        first + (core ^ half) * tok + lax.broadcasted_iota(jnp.int32, (1, tok), 1)
        for half in range(2)
    ]
    starts = [jnp.zeros_like(p) for p in pos]
    lows = [first * 0] * 2
    end = first * 0
    for d in range(doc_ref.shape[0]):
        end = end + doc_ref[d]
        lows = [jnp.where(first + i * tok >= end, end, low) for i, low in enumerate(lows)]
        starts = [jnp.where(p >= end, end, s) for p, s in zip(pos, starts)]
    return core, chip, pos, starts, lows


def blocks_back(chip, low, keys):
    return chip - low // keys + 1


def key_rows(core, tok):
    row = lax.broadcasted_iota(jnp.int32, (2 * tok, tok), 0)
    return ((row // tok) ^ core) * tok + lax.rem(row, tok)


def pieces(tok):
    for half in range(2):
        for c in range(PER_KV // 2):
            yield half, pl.ds(c * 2 * tok, 2 * tok), pl.ds((half * PER_KV + 2 * c) * tok, 2 * tok)


def softmax_step(k_tile, v_tile, q_rows, o_rows, bias, peak):
    scores = dot(k_tile, q_rows, NT) * TO_LOG2 + bias
    dprobs = dot(v_tile, o_rows, NT)
    top = jnp.max(scores, 0, keepdims=True)
    new_peak = top if peak is None else jnp.maximum(peak, top)
    weights = jnp.exp2(scores - new_peak)
    total = jnp.sum(weights, 0, keepdims=True)
    mixed = jnp.sum(weights * dprobs, 0, keepdims=True)
    return weights, dprobs, new_peak, total, mixed


def grad_terms(weights, dprobs, peak, stat_ref, cols):
    factor = jnp.exp2(peak - stat_ref[0:1, cols]) * stat_ref[1:2, cols]
    probs = weights * factor
    dscores = probs * (dprobs - stat_ref[2:3, cols])
    return probs.astype(jnp.bfloat16), dscores.astype(jnp.bfloat16)


def own_kernel(pairs, info_ref, doc_ref, *refs):
    blocks = refs[:GROUPS]
    sides = (refs[GROUPS : GROUPS + 2], refs[GROUPS + 2 : GROUPS + 4])
    qo_ref, kept_ref, stat_out, wide_s, sems = refs[GROUPS + 4 :]
    tok = blocks[0].shape[0] // 2
    width = PER_KV * HD
    mine_at = pl.multiple_of(lax.rem(info_ref[1], 2) * GROUPS * width, HD)
    runs = [(g, half, i) for g in range(GROUPS) for half in range(2) for i in range(2)]

    def wide(g, half, i):
        at = pl.multiple_of(mine_at + g * width, HD)
        return pltpu.make_async_copy(
            sides[half][i].at[:, pl.ds(at, width)], wide_s.at[g, half, i], sems.at[g, half, i]
        )

    for run in runs:
        wide(*run).start()
    core, chip, pos, starts, _ = place(info_ref, doc_ref, tok, pairs)
    key_pos = chip * 2 * tok + key_rows(core, tok)
    biases = []
    for half in range(2):
        bias = jnp.where((key_pos >= starts[half]) & (key_pos <= pos[half]), 0.0, -1e30)
        biases.append(jnp.concatenate([bias, bias], 1))
    for g in range(GROUPS):
        k_tile = blocks[g][:, K_COLS]
        v_tile = blocks[g][:, V_COLS]
        for half, rows, cols in pieces(tok):
            if rows.start == 0:
                for i in range(2):
                    wide(g, half, i).wait()
                    for h in range(PER_KV):
                        qo_ref[g, i, half, pl.ds(h * tok, tok), :] = wide_s[g, half, i, :, pl.ds(h * HD, HD)]
            weights, dprobs, peak, total, mixed = softmax_step(
                k_tile, v_tile, qo_ref[g, 0, half, rows, :], qo_ref[g, 1, half, rows, :], biases[half], None
            )
            kept_ref[g, 0, :, cols] = weights
            kept_ref[g, 1, :, cols] = dprobs
            stat_out[g, 0:1, cols] = peak
            stat_out[g, 1:2, cols] = total
            stat_out[g, 2:3, cols] = mixed


def reach_kernel(g, pairs, info_ref, doc_ref, qo_ref, first_stat, *refs):
    kv_refs = refs[: pairs + 1]
    refs = refs[-(2 * pairs + 3 + 4 - pairs) :]
    part_outs = refs[:pairs]
    ds_out, kv_all, stat_ref, weight_s, dprob_s, peak_s, dkv_s = refs[pairs:]
    keys = kv_refs[0].shape[0]
    tok = keys // 2
    pair = info_ref[1] // 2
    core, chip, _, starts, lows = place(info_ref, doc_ref, tok, pairs)
    count, later_count = (blocks_back(chip, low, keys) for low in lows)
    trim = (count == later_count) & (lax.rem(lows[0], keys) >= tok) & (count > 1)
    both_end = jnp.where(trim, later_count - 1, later_count)
    whole = pl.ds(0, keys)
    late_rows, early_rows = (pl.ds(pl.multiple_of((i ^ core) * tok, tok), tok) for i in (1, 0))
    half_cols = PER_KV * tok
    both = [(half, starts[half], rows, cols) for half, rows, cols in pieces(tok)]
    first_start = jnp.where(core == 0, starts[0], starts[1])
    one = [
        (core, first_start, pl.ds(at, keys), pl.ds(pl.multiple_of(core * half_cols + at, keys), keys))
        for at in range(0, half_cols, keys)
    ]

    kv_all[0] = kv_refs[0][...]
    kv_all[pairs] = kv_refs[pairs][...]
    for k in range(1, pairs):
        kv_all[distance(pair, k, pairs)] = kv_refs[k][...]
    dkv_s[...] = jnp.zeros_like(dkv_s)
    stat_ref[...] = first_stat[g]
    row = key_rows(core, tok)
    late = tok + lax.broadcasted_iota(jnp.int32, (tok, tok), 0)

    def stat_block(back, key_rows_, row_pos, todo):
        k_tile = kv_all[back, key_rows_, K_COLS]
        v_tile = kv_all[back, key_rows_, V_COLS]
        key_pos = (chip - back) * keys + row_pos
        biases = {}
        for half, start, rows, cols in todo:
            if id(start) not in biases:
                bias = jnp.where(key_pos >= start, 0.0, -1e30)
                biases[id(start)] = jnp.concatenate([bias, bias], 1)
            old = stat_ref[0:1, cols]
            weights, dprobs, peak, total, mixed = softmax_step(
                k_tile, v_tile, qo_ref[g, 0, half, rows, :], qo_ref[g, 1, half, rows, :], biases[id(start)], old
            )
            rescale = jnp.exp2(old - peak)
            stat_ref[0:1, cols] = peak
            stat_ref[1:2, cols] = stat_ref[1:2, cols] * rescale + total
            stat_ref[2:3, cols] = stat_ref[2:3, cols] * rescale + mixed
            weight_s[back - 1, key_rows_, cols] = weights
            dprob_s[back - 1, key_rows_, cols] = dprobs
            peak_s[back - 1, :, cols] = peak

    def each(start, end, work):
        def step(back, carry):
            work(back)
            return carry

        lax.fori_loop(start, end, step, 0)

    each(1, both_end, lambda back: stat_block(back, whole, row, both))
    each(later_count, count, lambda back: stat_block(back, whole, row, one))

    @pl.when(trim)
    def _():
        stat_block(count - 1, late_rows, late, both)

    inv_total = 1.0 / stat_ref[1:2, :]
    stat_ref[1:2, :] = inv_total
    stat_ref[2:3, :] = stat_ref[2:3, :] * inv_total

    def grad_block(back, key_rows_, todo):
        dk = jnp.zeros((key_rows_.size, HD), jnp.float32)
        dv = jnp.zeros((key_rows_.size, HD), jnp.float32)
        for half, _, rows, cols in todo:
            probs_b, dscores = grad_terms(
                weight_s[back - 1, key_rows_, cols],
                dprob_s[back - 1, key_rows_, cols],
                peak_s[back - 1, :, cols],
                stat_ref,
                cols,
            )
            dv = dv + dot(probs_b, qo_ref[g, 1, half, rows, :], NN)
            dk = dk + dot(dscores, qo_ref[g, 0, half, rows, :], NN)
            ds_out[back - 1, key_rows_, cols] = dscores
        dkv_s[back - 1, key_rows_, K_COLS] = (dk * INV_ROOT).astype(jnp.bfloat16)
        dkv_s[back - 1, key_rows_, V_COLS] = dv.astype(jnp.bfloat16)

    def one_side(back):
        grad_block(back, whole, one)
        unused = pl.ds(pl.multiple_of((1 - core) * half_cols, half_cols), half_cols)
        ds_out[back - 1, :, unused] = jnp.zeros((keys, half_cols), jnp.bfloat16)

    each(1, both_end, lambda back: grad_block(back, whole, both))
    each(later_count, count, one_side)

    @pl.when(trim)
    def _():
        grad_block(count - 1, late_rows, both)
        ds_out[count - 2, early_rows, :] = jnp.zeros((tok, 2 * half_cols), jnp.bfloat16)

    part_outs[pairs - 1][...] = dkv_s[pairs - 1]
    for k in range(1, pairs):
        part_outs[k - 1][...] = dkv_s[distance(pair, k, pairs) - 1]


def rest_kernel(
    g, pairs, info_ref, doc_ref, qo_ref, kept_ref, first_stat, stat_ref, ds_ref, kv_ref, *refs
):
    own_out, dq_mine, dq_theirs, dq_s = refs[-4:]
    keys = kv_ref.shape[1]
    tok = keys // 2
    _, chip, _, _, lows = place(info_ref, doc_ref, tok, pairs)
    count = blocks_back(chip, lows[0], keys)
    k_tile = kv_ref[0, :, K_COLS]
    dk = jnp.zeros((keys, HD), jnp.float32)
    dv = jnp.zeros((keys, HD), jnp.float32)
    for half, rows, cols in pieces(tok):
        probs_b, dscores = grad_terms(
            kept_ref[g, 0, :, cols], kept_ref[g, 1, :, cols], first_stat[g, 0:1, cols], stat_ref, cols
        )
        dv = dv + dot(probs_b, qo_ref[g, 1, half, rows, :], NN)
        dk = dk + dot(dscores, qo_ref[g, 0, half, rows, :], NN)
        dq_s[:, cols] = dot(k_tile, dscores, TN)
    own_out[:, K_COLS] = dk * INV_ROOT
    own_out[:, V_COLS] = dv

    def query_step(back, carry):
        k_tile = kv_ref[back, :, K_COLS]
        for half, rows, cols in pieces(tok):
            dq_s[:, cols] += dot(k_tile, ds_ref[back - 1, :, cols], TN)
        return carry

    lax.fori_loop(1, count, query_step, 0)
    for half, dq_ref in enumerate((dq_mine, dq_theirs)):
        for h in range(PER_KV):
            block = dq_s[:, pl.ds((half * PER_KV + h) * tok, tok)] * INV_ROOT
            dq_ref[:, pl.ds(h * HD, HD)] = block.T.astype(jnp.bfloat16)


def finish_kernel(tok, info_ref, *refs):
    own = refs[:GROUPS]
    back = refs[GROUPS : 2 * GROUPS]
    own_other = refs[2 * GROUPS]
    back_other = refs[2 * GROUPS + 1 : 3 * GROUPS + 1]
    grad_k, grad_v = refs[3 * GROUPS + 1 :]
    core = lax.rem(info_ref[1], 2)
    for g in range(GROUPS):
        mine = own[g][:tok] + back[g][:tok].astype(jnp.float32)
        other = own_other[g] + back_other[g][tok:].astype(jnp.float32)
        for total, side in ((mine, core), (other, 1 - core)):
            cols = pl.ds(pl.multiple_of((side * GROUPS + g) * HD, HD), HD)
            grad_k[:, cols] = total[:, :HD].astype(jnp.bfloat16)
            grad_v[:, cols] = total[:, HD:].astype(jnp.bfloat16)


def nbytes(shapes):
    total = 0
    for s in shapes:
        size = jnp.dtype(s.dtype).itemsize
        for n in s.shape:
            size *= n
        total += size
    return total


def call(kernel, name, scalars, arrays, out_shape, scratch=(), flops=0, passing=(), hbm=(), sems=None):
    smem = pl.BlockSpec(memory_space=pltpu.SMEM)
    vmem = pl.BlockSpec(memory_space=pltpu.VMEM)
    used = nbytes(arrays) + nbytes(out_shape) + nbytes(scratch)
    return pl.pallas_call(
        kernel,
        out_shape=out_shape,
        in_specs=[smem] * len(scalars)
        + [vmem] * len(arrays)
        + [pl.BlockSpec(memory_space=pl.ANY)] * (len(hbm) + len(passing)),
        out_specs=[vmem] * len(out_shape),
        scratch_shapes=[pltpu.VMEM(s.shape, s.dtype) for s in scratch]
        + ([pltpu.SemaphoreType.DMA(sems)] if sems else []),
        compiler_params=pltpu.CompilerParams(vmem_limit_bytes=used + 3 * MIB),
        cost_estimate=pl.CostEstimate(
            flops=flops, bytes_accessed=nbytes(arrays) + nbytes(out_shape), transcendentals=0
        ),
        name=name,
    )(*scalars, *arrays, *hbm, *passing)


def local(queries, keys, values, grad_out, doc_lengths):
    tok = queries.shape[0]
    dp_count = lax.axis_size("dp")
    seq_count = lax.axis_size("seq")
    pairs = seq_count // 2
    dp_idx = lax.axis_index("dp")
    seq_idx = lax.axis_index("seq")
    core = lax.rem(seq_idx, 2)
    pair = seq_idx // 2
    rows = 2 * tok
    lanes = 2 * PER_KV * tok
    f32, bf16 = jnp.float32, jnp.bfloat16
    shape = jax.ShapeDtypeStruct

    def swap(value, k):
        return lax.ppermute(value, "seq", [(i, i ^ k) for i in range(seq_count)])

    k_theirs = swap(keys, 1)
    v_theirs = swap(values, 1)

    def block(g):
        at = (core * GROUPS + g) * HD
        cut = [
            [lax.dynamic_slice_in_dim(t, at, HD, 1) for t in side]
            for side in ((keys, values), (k_theirs, v_theirs))
        ]
        return jnp.concatenate([jnp.concatenate(side, 1) for side in cut], 0)

    own = [block(g) for g in range(GROUPS)]
    prev = [lax.ppermute(o, "dp", [(i, (i + 1) % dp_count) for i in range(dp_count)]) for o in own]
    q_sent, o_sent, _ = lax.optimization_barrier((queries, grad_out, own[-1]))
    q_theirs, o_theirs = swap(q_sent, 1), swap(o_sent, 1)
    info = jnp.stack([dp_idx, seq_idx]).astype(jnp.int32)
    scalars = [info, doc_lengths]

    blocks = []
    for g in range(GROUPS):
        own_now, prev_now = own[g], prev[g]
        if g:
            own_now, *_ = lax.optimization_barrier((own_now, *chosen))
        chosen = [jnp.where((pair ^ k) > pair, own_now, prev_now) for k in range(1, pairs)]
        sent = [swap(c, 2 * k) for k, c in enumerate(chosen, 1)]
        blocks.append([own[g]] + sent + [prev[g]])

    stat = shape((3, lanes), f32)
    unit = 2 * rows * lanes * HD
    outs = call(
        functools.partial(own_kernel, pairs),
        "own",
        scalars,
        own,
        [
            shape((GROUPS, 2, 2, PER_KV * tok, HD), bf16),
            shape((GROUPS, 2, rows, lanes), f32),
            shape((GROUPS, 3, lanes), f32),
        ],
        flops=2 * GROUPS * unit,
        hbm=[queries, grad_out, q_theirs, o_theirs],
        scratch=[shape((GROUPS, 2, 2, tok, PER_KV * HD), bf16)],
        sems=(GROUPS, 2, 2),
    )
    qo, kept, first_stats = outs

    part = shape((rows, 2 * HD), bf16)
    reached, own_parts = [], []
    for g in range(GROUPS):
        stats = first_stats
        if g:
            stats, _ = lax.optimization_barrier((stats, reached[-1][pairs + 2]))
        reached.append(
            call(
                functools.partial(reach_kernel, g, pairs),
                "reach_%d" % g,
                scalars,
                [qo, stats] + blocks[g],
                [part] * pairs
                + [shape((pairs, rows, lanes), bf16), shape((pairs + 1, rows, 2 * HD), bf16), stat],
                [
                    shape((pairs, rows, lanes), f32),
                    shape((pairs, rows, lanes), f32),
                    shape((pairs, 1, lanes), f32),
                    shape((pairs, rows, 2 * HD), bf16),
                ],
                flops=4 * pairs * unit,
                passing=[kept] + [r[pairs] for r in reached],
            )
        )
    own_sums, backs, marks = [], [], []
    for g in range(GROUPS):
        prev_sum = reached[g][pairs - 1].astype(f32)
        own_sum = 0.0
        received = [swap(reached[g][k - 1], 2 * k) for k in range(1, pairs)]
        for k in range(1, pairs):
            back = received[k - 1].astype(f32)
            later = (pair ^ k) > pair
            own_sum = own_sum + jnp.where(later, back, 0.0)
            prev_sum = prev_sum + jnp.where(later, 0.0, back)
        own_sums.append(own_sum)
        prev_sum = prev_sum.astype(bf16)
        marks.append(prev_sum)
        backs.append(
            lax.ppermute(
                prev_sum, "dp", [((i + 1) % dp_count, i) for i in range(dp_count)]
            )
        )
    dq_mine, dq_other = [], []
    for g in range(GROUPS):
        ds, kv, stats = reached[g][pairs:]
        stats, _ = lax.optimization_barrier((stats, marks[g]))
        dq_shape = shape((tok, PER_KV * HD), bf16)
        own_part, mine, theirs = call(
            functools.partial(rest_kernel, g, pairs),
            "rest_%d" % g,
            scalars,
            [qo, kept, first_stats, stats, ds, kv],
            [shape((rows, 2 * HD), f32), dq_shape, dq_shape],
            [shape((HD, lanes), f32)],
            flops=(3 + pairs) * unit,
            passing=[r[pairs] for r in reached[g + 1 :]],
        )
        own_sums[g] = own_sums[g] + own_part
        dq_mine.append(mine)
        dq_other.append(swap(theirs, 1))
    own_other = swap(jnp.stack([t[tok:] for t in own_sums]), 1)
    low = [jnp.where(core == 0, x, y) for x, y in zip(dq_mine, dq_other)]
    high = [jnp.where(core == 0, y, x) for x, y in zip(dq_mine, dq_other)]
    grad_q = jnp.concatenate(low + high, 1)
    grad_q, own_other, backs[-1] = lax.optimization_barrier((grad_q, own_other, backs[-1]))
    back_other = [swap(b, 1) for b in backs]
    out = shape((tok, KVH * HD), bf16)
    grad_k, grad_v = call(
        functools.partial(finish_kernel, tok),
        "finish",
        [info],
        own_sums + backs + [own_other] + back_other,
        [out, out],
    )
    return (grad_q, grad_k, grad_v)


def solution(mesh):
    spec = P(("dp", "seq"), None)
    return jax.shard_map(
        local,
        mesh=mesh,
        in_specs=(spec, spec, spec, spec, P()),
        out_specs=(spec, spec, spec),
        check_vma=False,
    )
```

profile of v0, /device:TPU:0, one launch (start us, length us, event | category | flops | bytes accessed | tf_op | source)
XLA Modules:
  0.0 55.7 jit_solution(7123003154716485156)
XLA Ops:
  1.3 0.8 %constant_dynamic-slice_fusion.2 = (bf16[128,128]{1,0:T(8,128)(2,1)S(1)}, bf16[128,128]{1,0:T(8,128)(2,1)S(1)}, bf16[128,128]{1,0:T(8,128)(2,1)S(1)}, bf16[128,128]{1,0:T(8,128)(2,1)S(1)}) fusion(bf16[128,512]{1,0:T(8,128)(2,1)} %param.7, s32[]{:T(128)S(6)} %select_n.123, s32[]{:T(128)S(6)} %select_n.122, bf16[128,512]{1,0:T(8,128)(2,1)} %param.6), kind=kLoop, calls=%fused_computation.44 | loop fusion | bytes 262152 | tf_op jit(solution)/shard_map/dynamic_slice | solution.py:335
  3.4 2.8 %collective-permute-start.4 = (bf16[256,256]{1,0:T(8,128)(2,1)S(1)}, bf16[256,256]{1,0:T(8,128)(2,1)S(1)}, u32[]{:S(2)}, u32[]{:S(2)}) collective-permute-start(bf16[256,256]{1,0:T(8,128)(2,1)S(1)} %maximum_maximum_fusion.refs_0_), channel_id=1, source_target_pairs={{0,8},{8,16},{16,24},{24,0},{1,9},{9,17},{17,25},{25,1},{2,10},{10... | collective-permute-start | bytes 393224 | tf_op jit(solution)/shard_map/ppermute | solution.py:341
  6.3 1.6 %collective-permute-start.11 = (bf16[256,256]{1,0:T(8,128)(2,1)S(1)}, bf16[256,256]{1,0:T(8,128)(2,1)S(1)}, u32[]{:S(2)}, u32[]{:S(2)}) collective-permute-start(bf16[256,256]{1,0:T(8,128)(2,1)S(1)} %maximum_maximum_fusion.1.refs_1_.refs_0_), channel_id=1, source_target_pairs={{0,8},{8,16},{16,24},{24,0},{1,9},{9,17},{17,25},{25,1},{2,10},{10... | collective-permute-start | bytes 393224 | tf_op jit(solution)/shard_map/ppermute | solution.py:341
  7.8 4.6 %collective-permute-done.4.refs_4_ = bf16[256,256]{1,0:T(8,128)(2,1)S(1)} collective-permute-done((bf16[256,256]{1,0:T(8,128)(2,1)S(1)}, bf16[256,256]{1,0:T(8,128)(2,1)S(1)}, u32[]{:S(2)}, u32[]{:S(2)}) %collective-permute-start.4) | collective-permute-done | bytes 131104 | tf_op jit(solution)/shard_map/ppermute | solution.py:341
  12.5 1.8 %collective-permute-start.5 = (bf16[256,256]{1,0:T(8,128)(2,1)S(1)}, bf16[256,256]{1,0:T(8,128)(2,1)S(1)}, u32[]{:S(2)}, u32[]{:S(2)}) collective-permute-start(bf16[256,256]{1,0:T(8,128)(2,1)S(1)} %get-tuple-element.80), channel_id=1, source_target_pairs={{0,2},{1,3},{2,0},{3,1},{4,6},{5,7},{6,4},{7,5},{8,10},{9,11},{10,... | collective-permute-start | bytes 393224 | tf_op jit(solution)/shard_map/ppermute | solution.py:327
  14.3 1.5 %collective-permute-start.6 = (bf16[256,256]{1,0:T(8,128)(2,1)S(1)}, bf16[256,256]{1,0:T(8,128)(2,1)S(1)}, u32[]{:S(2)}, u32[]{:S(2)}) collective-permute-start(bf16[256,256]{1,0:T(8,128)(2,1)S(1)} %get-tuple-element.79), channel_id=1, source_target_pairs={{0,4},{1,5},{2,6},{3,7},{4,0},{5,1},{6,2},{7,3},{8,12},{9,13},{10,... | collective-permute-start | bytes 393224 | tf_op jit(solution)/shard_map/ppermute | solution.py:327
  15.9 1.6 %collective-permute-start.7 = (bf16[256,256]{1,0:T(8,128)(2,1)S(1)}, bf16[256,256]{1,0:T(8,128)(2,1)S(1)}, u32[]{:S(2)}, u32[]{:S(2)}) collective-permute-start(bf16[256,256]{1,0:T(8,128)(2,1)S(1)} %get-tuple-element.78), channel_id=1, source_target_pairs={{0,6},{1,7},{2,4},{3,5},{4,2},{5,3},{6,0},{7,1},{8,14},{9,15},{10,... | collective-permute-start | bytes 393224 | tf_op jit(solution)/shard_map/ppermute | solution.py:327
  17.5 0.6 %collective-permute-start.12 = (bf16[256,256]{1,0:T(8,128)(2,1)S(1)}, bf16[256,256]{1,0:T(8,128)(2,1)S(1)}, u32[]{:S(2)}, u32[]{:S(2)}) collective-permute-start(bf16[256,256]{1,0:T(8,128)(2,1)S(1)} %get-tuple-element.77), channel_id=1, source_target_pairs={{0,2},{1,3},{2,0},{3,1},{4,6},{5,7},{6,4},{7,5},{8,10},{9,11},{10,... | collective-permute-start | bytes 393224 | tf_op jit(solution)/shard_map/ppermute | solution.py:327
  18.1 1.4 %collective-permute-start.13 = (bf16[256,256]{1,0:T(8,128)(2,1)S(1)}, bf16[256,256]{1,0:T(8,128)(2,1)S(1)}, u32[]{:S(2)}, u32[]{:S(2)}) collective-permute-start(bf16[256,256]{1,0:T(8,128)(2,1)S(1)} %get-tuple-element.76), channel_id=1, source_target_pairs={{0,4},{1,5},{2,6},{3,7},{4,0},{5,1},{6,2},{7,3},{8,12},{9,13},{10,... | collective-permute-start | bytes 393224 | tf_op jit(solution)/shard_map/ppermute | solution.py:327
  19.5 3.5 %own.1 = (bf16[2,2,2,1024,128]{4,3,2,1,0:T(8,128)(2,1)S(1)}, f32[2,2,256,2048]{3,2,1,0:T(8,128)S(1)}, f32[2,3,2048]{2,1,0:T(4,128)S(1)}) custom-call(s32[2]{0:T(128)S(1)} %pad_add_fusion.info_ref, s32[16]{0:T(128)S(1)} %copy-done.2, bf16[256,256]{1,0:T(8,128)(2,1)S(1)} %maximum_maximum_fusion.refs_0_, ...), custom_call_target="tpu_custom_call" | custom-call | flops 536870912 | bytes 10797056 | tf_op jit(solution)/shard_map/own/pallas_call | solution.py:295
  23.0 1.6 %collective-permute-start.14 = (bf16[256,256]{1,0:T(8,128)(2,1)S(1)}, bf16[256,256]{1,0:T(8,128)(2,1)S(1)}, u32[]{:S(2)}, u32[]{:S(2)}) collective-permute-start(bf16[256,256]{1,0:T(8,128)(2,1)S(1)} %get-tuple-element.75), channel_id=1, source_target_pairs={{0,6},{1,7},{2,4},{3,5},{4,2},{5,3},{6,0},{7,1},{8,14},{9,15},{10,... | collective-permute-start | bytes 393224 | tf_op jit(solution)/shard_map/ppermute | solution.py:327
  24.7 0.7 %reach_0.1 = (bf16[256,256]{1,0:T(8,128)(2,1)S(1)}, bf16[256,256]{1,0:T(8,128)(2,1)S(1)}, bf16[256,256]{1,0:T(8,128)(2,1)S(1)}, bf16[256,256]{1,0:T(8,128)(2,1)S...) custom-call(s32[2]{0:T(128)S(1)} %pad_add_fusion.info_ref, ...), custom_call_target="tpu_custom_call" | custom-call | flops 2147483648 | bytes 8200192 | tf_op jit(solution)/shard_map/reach_0/pallas_call | solution.py:295
  25.4 6.5 %collective-permute-start.10 = (bf16[256,256]{1,0:T(8,128)(2,1)S(1)}, bf16[256,256]{1,0:T(8,128)(2,1)S(1)}, u32[]{:S(2)}, u32[]{:S(2)}) collective-permute-start(bf16[256,256]{1,0:T(8,128)(2,1)S(1)} %get-tuple-element.46), channel_id=1, source_target_pairs={{0,6},{1,7},{2,4},{3,5},{4,2},{5,3},{6,0},{7,1},{8,14},{9,15},{10,... | collective-permute-start | bytes 393224 | tf_op jit(solution)/shard_map/ppermute | solution.py:327
  31.9 0.6 %collective-permute-start.9 = (bf16[256,256]{1,0:T(8,128)(2,1)S(1)}, bf16[256,256]{1,0:T(8,128)(2,1)S(1)}, u32[]{:S(2)}, u32[]{:S(2)}) collective-permute-start(bf16[256,256]{1,0:T(8,128)(2,1)S(1)} %get-tuple-element.45), channel_id=1, source_target_pairs={{0,4},{1,5},{2,6},{3,7},{4,0},{5,1},{6,2},{7,3},{8,12},{9,13},{10,... | collective-permute-start | bytes 393224 | tf_op jit(solution)/shard_map/ppermute | solution.py:327
  32.6 0.9 %reach_1.1 = (bf16[256,256]{1,0:T(8,128)(2,1)S(1)}, bf16[256,256]{1,0:T(8,128)(2,1)S(1)}, bf16[256,256]{1,0:T(8,128)(2,1)S(1)}, bf16[256,256]{1,0:T(8,128)(2,1)S...) custom-call(s32[2]{0:T(128)S(1)} %pad_add_fusion.info_ref, ...), custom_call_target="tpu_custom_call" | custom-call | flops 2147483648 | bytes 8200192 | tf_op jit(solution)/shard_map/reach_1/pallas_call | solution.py:295
  33.5 3.2 %collective-permute-start.16 = (bf16[256,256]{1,0:T(8,128)(2,1)S(1)}, bf16[256,256]{1,0:T(8,128)(2,1)S(1)}, u32[]{:S(2)}, u32[]{:S(2)}) collective-permute-start(bf16[256,256]{1,0:T(8,128)(2,1)S(1)} %get-tuple-element.57), channel_id=1, source_target_pairs={{0,2},{1,3},{2,0},{3,1},{4,6},{5,7},{6,4},{7,5},{8,10},{9,11},{10,... | collective-permute-start | bytes 393224 | tf_op jit(solution)/shard_map/ppermute | solution.py:327
  36.6 5.4 %collective-permute-start.17 = (bf16[256,256]{1,0:T(8,128)(2,1)S(1)}, bf16[256,256]{1,0:T(8,128)(2,1)S(1)}, u32[]{:S(2)}, u32[]{:S(2)}) collective-permute-start(bf16[256,256]{1,0:T(8,128)(2,1)S(1)} %get-tuple-element.58), channel_id=1, source_target_pairs={{0,4},{1,5},{2,6},{3,7},{4,0},{5,1},{6,2},{7,3},{8,12},{9,13},{10,... | collective-permute-start | bytes 393224 | tf_op jit(solution)/shard_map/ppermute | solution.py:327
  42.2 1.6 %rest_0.1 = (f32[256,256]{1,0:T(8,128)S(1)}, bf16[128,1024]{1,0:T(8,128)(2,1)S(1)}, bf16[128,1024]{1,0:T(8,128)(2,1)S(1)}) custom-call(s32[2]{0:T(128)S(1)} %pad_add_fusion.info_ref, s32[16]{0:T(128)S(1)} %copy-done.2, bf16[2,2,2,1024,128]{4,3,2,1,0:T(8,128)(2,1)S(1)} %get-tuple-element.39.qo_ref, ...), custom_call_target="tpu_custom_call" | custom-call | flops 939524096 | bytes 16195584 | tf_op jit(solution)/shard_map/rest_0/pallas_call | solution.py:295
  44.0 2.0 %collective-permute-done.17 = bf16[256,256]{1,0:T(8,128)(2,1)S(1)} collective-permute-done((bf16[256,256]{1,0:T(8,128)(2,1)S(1)}, bf16[256,256]{1,0:T(8,128)(2,1)S(1)}, u32[]{:S(2)}, u32[]{:S(2)}) %collective-permute-start.17) | collective-permute-done | bytes 131104 | tf_op jit(solution)/shard_map/ppermute | solution.py:327
  45.9 1.9 %collective-permute-done.18 = bf16[256,256]{1,0:T(8,128)(2,1)S(1)} collective-permute-done((bf16[256,256]{1,0:T(8,128)(2,1)S(1)}, bf16[256,256]{1,0:T(8,128)(2,1)S(1)}, u32[]{:S(2)}, u32[]{:S(2)}) %collective-permute-start.18) | collective-permute-done | bytes 131104 | tf_op jit(solution)/shard_map/ppermute | solution.py:327
  48.1 1.6 %rest_1.1 = (f32[256,256]{1,0:T(8,128)S(1)}, bf16[128,1024]{1,0:T(8,128)(2,1)S(1)}, bf16[128,1024]{1,0:T(8,128)(2,1)S(1)}) custom-call(s32[2]{0:T(128)S(1)} %pad_add_fusion.info_ref, s32[16]{0:T(128)S(1)} %copy-done.2, bf16[2,2,2,1024,128]{4,3,2,1,0:T(8,128)(2,1)S(1)} %get-tuple-element.39.qo_ref, ...), custom_call_target="tpu_custom_call" | custom-call | flops 939524096 | bytes 16195584 | tf_op jit(solution)/shard_map/rest_1/pallas_call | solution.py:295
  51.7 1.0 %pad_maximum_fusion = bf16[128,4096]{1,0:T(8,128)(2,1)} fusion(bf16[128,1024]{1,0:T(8,128)(2,1)S(1)} %get-tuple-element.74, bf16[128,1024]{1,0:T(8,128)(2,1)S(1)} %get-tuple-element.72, bf16[128,1024]{1,0:T(8,128)(2,1)S(1)} %get-tuple-element.73, bf16[128,1024]{1,0:T(8,128)(2,1)S(1)} %get-tuple-element.71), kind=kLoop, calls=%fused_computation | loop fusion | flops 4194304 | bytes 2097152 | tf_op jit(solution)/shard_map/concatenate | solution.py:438
  53.1 1.3 %collective-permute-done.24.refs_6_ = bf16[256,256]{1,0:T(8,128)(2,1)S(1)} collective-permute-done((bf16[256,256]{1,0:T(8,128)(2,1)S(1)}, bf16[256,256]{1,0:T(8,128)(2,1)S(1)}, u32[]{:S(2)}, u32[]{:S(2)}) %collective-permute-start.24) | collective-permute-done | bytes 131104 | tf_op jit(solution)/shard_map/ppermute | solution.py:327
  54.4 1.3 %finish.1 = (bf16[128,512]{1,0:T(8,128)(2,1)}, bf16[128,512]{1,0:T(8,128)(2,1)}) custom-call(s32[2]{0:T(128)S(1)} %pad_add_fusion.info_ref, f32[256,256]{1,0:T(8,128)S(1)} %fusion.6.refs_0_, f32[256,256]{1,0:T(8,128)S(1)} %fusion.13.refs_1_, bf16[256,256]{1,0:T(8,128)(2,1)S(1)} %collective-permute-done.22.refs_2_, ...), custom_call_target="tpu_custom_call" | custom-call | bytes 1572864 | tf_op jit(solution)/shard_map/finish/pallas_call | solution.py:295
  (56 shorter events, 4.8 us)
Async XLA Ops:
  0.7 1.7 %collective-permute-start = (bf16[128,512]{1,0:T(8,128)(2,1)}, bf16[128,512]{1,0:T(8,128)(2,1)S(1)}, u32[]{:S(2)}, u32[]{:S(2)}) collective-permute-start(bf16[128,512]{1,0:T(8,128)(2,1)} %param.6), channel_id=1, source_target_pairs={{0,1},{1,0},{2,3},{3,2},{4,5},{5,4},{6,7},{7,6},{8,9},{9,8},{10,11... | collective-permute-start | bytes 393224 | tf_op jit(solution)/shard_map/ppermute | solution.py:327
  1.2 1.6 %collective-permute-start.1 = (bf16[128,512]{1,0:T(8,128)(2,1)}, bf16[128,512]{1,0:T(8,128)(2,1)S(1)}, u32[]{:S(2)}, u32[]{:S(2)}) collective-permute-start(bf16[128,512]{1,0:T(8,128)(2,1)} %param.7), channel_id=1, source_target_pairs={{0,1},{1,0},{2,3},{3,2},{4,5},{5,4},{6,7},{7,6},{8,9},{9,8},{10,11... | collective-permute-start | bytes 393224 | tf_op jit(solution)/shard_map/ppermute | solution.py:327
  2.8 14.7 %collective-permute-start.2 = (bf16[128,4096]{1,0:T(8,128)(2,1)}, bf16[128,4096]{1,0:T(8,128)(2,1)}, u32[]{:S(2)}, u32[]{:S(2)}) collective-permute-start(bf16[128,4096]{1,0:T(8,128)(2,1)} %refs_2_.1), channel_id=1, source_target_pairs={{0,1},{1,0},{2,3},{3,2},{4,5},{5,4},{6,7},{7,6},{8,9},{9,8},{10,11... | collective-permute-start | bytes 3145736 | tf_op jit(solution)/shard_map/ppermute | solution.py:327
  3.0 15.1 %collective-permute-start.3 = (bf16[128,4096]{1,0:T(8,128)(2,1)}, bf16[128,4096]{1,0:T(8,128)(2,1)}, u32[]{:S(2)}, u32[]{:S(2)}) collective-permute-start(bf16[128,4096]{1,0:T(8,128)(2,1)} %refs_3_.1), channel_id=1, source_target_pairs={{0,1},{1,0},{2,3},{3,2},{4,5},{5,4},{6,7},{7,6},{8,9},{9,8},{10,11... | collective-permute-start | bytes 3145736 | tf_op jit(solution)/shard_map/ppermute | solution.py:327
  3.4 9.1 %collective-permute-start.4 = (bf16[256,256]{1,0:T(8,128)(2,1)S(1)}, bf16[256,256]{1,0:T(8,128)(2,1)S(1)}, u32[]{:S(2)}, u32[]{:S(2)}) collective-permute-start(bf16[256,256]{1,0:T(8,128)(2,1)S(1)} %maximum_maximum_fusion.refs_0_), channel_id=1, source_target_pairs={{0,8},{8,16},{16,24},{24,0},{1,9},{9,17},{17,25},{25,1},{2,10},{10... | collective-permute-start | bytes 393224 | tf_op jit(solution)/shard_map/ppermute | solution.py:341
  6.3 9.6 %collective-permute-start.11 = (bf16[256,256]{1,0:T(8,128)(2,1)S(1)}, bf16[256,256]{1,0:T(8,128)(2,1)S(1)}, u32[]{:S(2)}, u32[]{:S(2)}) collective-permute-start(bf16[256,256]{1,0:T(8,128)(2,1)S(1)} %maximum_maximum_fusion.1.refs_1_.refs_0_), channel_id=1, source_target_pairs={{0,8},{8,16},{16,24},{24,0},{1,9},{9,17},{17,25},{25,1},{2,10},{10... | collective-permute-start | bytes 393224 | tf_op jit(solution)/shard_map/ppermute | solution.py:341
  12.5 10.5 %collective-permute-start.5 = (bf16[256,256]{1,0:T(8,128)(2,1)S(1)}, bf16[256,256]{1,0:T(8,128)(2,1)S(1)}, u32[]{:S(2)}, u32[]{:S(2)}) collective-permute-start(bf16[256,256]{1,0:T(8,128)(2,1)S(1)} %get-tuple-element.80), channel_id=1, source_target_pairs={{0,2},{1,3},{2,0},{3,1},{4,6},{5,7},{6,4},{7,5},{8,10},{9,11},{10,... | collective-permute-start | bytes 393224 | tf_op jit(solution)/shard_map/ppermute | solution.py:327
  14.3 10.3 %collective-permute-start.6 = (bf16[256,256]{1,0:T(8,128)(2,1)S(1)}, bf16[256,256]{1,0:T(8,128)(2,1)S(1)}, u32[]{:S(2)}, u32[]{:S(2)}) collective-permute-start(bf16[256,256]{1,0:T(8,128)(2,1)S(1)} %get-tuple-element.79), channel_id=1, source_target_pairs={{0,4},{1,5},{2,6},{3,7},{4,0},{5,1},{6,2},{7,3},{8,12},{9,13},{10,... | collective-permute-start | bytes 393224 | tf_op jit(solution)/shard_map/ppermute | solution.py:327
  15.9 8.8 %collective-permute-start.7 = (bf16[256,256]{1,0:T(8,128)(2,1)S(1)}, bf16[256,256]{1,0:T(8,128)(2,1)S(1)}, u32[]{:S(2)}, u32[]{:S(2)}) collective-permute-start(bf16[256,256]{1,0:T(8,128)(2,1)S(1)} %get-tuple-element.78), channel_id=1, source_target_pairs={{0,6},{1,7},{2,4},{3,5},{4,2},{5,3},{6,0},{7,1},{8,14},{9,15},{10,... | collective-permute-start | bytes 393224 | tf_op jit(solution)/shard_map/ppermute | solution.py:327
  17.5 14.4 %collective-permute-start.12 = (bf16[256,256]{1,0:T(8,128)(2,1)S(1)}, bf16[256,256]{1,0:T(8,128)(2,1)S(1)}, u32[]{:S(2)}, u32[]{:S(2)}) collective-permute-start(bf16[256,256]{1,0:T(8,128)(2,1)S(1)} %get-tuple-element.77), channel_id=1, source_target_pairs={{0,2},{1,3},{2,0},{3,1},{4,6},{5,7},{6,4},{7,5},{8,10},{9,11},{10,... | collective-permute-start | bytes 393224 | tf_op jit(solution)/shard_map/ppermute | solution.py:327
  18.1 14.4 %collective-permute-start.13 = (bf16[256,256]{1,0:T(8,128)(2,1)S(1)}, bf16[256,256]{1,0:T(8,128)(2,1)S(1)}, u32[]{:S(2)}, u32[]{:S(2)}) collective-permute-start(bf16[256,256]{1,0:T(8,128)(2,1)S(1)} %get-tuple-element.76), channel_id=1, source_target_pairs={{0,4},{1,5},{2,6},{3,7},{4,0},{5,1},{6,2},{7,3},{8,12},{9,13},{10,... | collective-permute-start | bytes 393224 | tf_op jit(solution)/shard_map/ppermute | solution.py:327
  23.0 9.5 %collective-permute-start.14 = (bf16[256,256]{1,0:T(8,128)(2,1)S(1)}, bf16[256,256]{1,0:T(8,128)(2,1)S(1)}, u32[]{:S(2)}, u32[]{:S(2)}) collective-permute-start(bf16[256,256]{1,0:T(8,128)(2,1)S(1)} %get-tuple-element.75), channel_id=1, source_target_pairs={{0,6},{1,7},{2,4},{3,5},{4,2},{5,3},{6,0},{7,1},{8,14},{9,15},{10,... | collective-permute-start | bytes 393224 | tf_op jit(solution)/shard_map/ppermute | solution.py:327
  25.4 16.6 %collective-permute-start.10 = (bf16[256,256]{1,0:T(8,128)(2,1)S(1)}, bf16[256,256]{1,0:T(8,128)(2,1)S(1)}, u32[]{:S(2)}, u32[]{:S(2)}) collective-permute-start(bf16[256,256]{1,0:T(8,128)(2,1)S(1)} %get-tuple-element.46), channel_id=1, source_target_pairs={{0,6},{1,7},{2,4},{3,5},{4,2},{5,3},{6,0},{7,1},{8,14},{9,15},{10,... | collective-permute-start | bytes 393224 | tf_op jit(solution)/shard_map/ppermute | solution.py:327
  31.9 10.1 %collective-permute-start.8 = (bf16[256,256]{1,0:T(8,128)(2,1)S(1)}, bf16[256,256]{1,0:T(8,128)(2,1)S(1)}, u32[]{:S(2)}, u32[]{:S(2)}) collective-permute-start(bf16[256,256]{1,0:T(8,128)(2,1)S(1)} %get-tuple-element.44), channel_id=1, source_target_pairs={{0,2},{1,3},{2,0},{3,1},{4,6},{5,7},{6,4},{7,5},{8,10},{9,11},{10,... | collective-permute-start | bytes 393224 | tf_op jit(solution)/shard_map/ppermute | solution.py:327
  31.9 10.1 %collective-permute-start.9 = (bf16[256,256]{1,0:T(8,128)(2,1)S(1)}, bf16[256,256]{1,0:T(8,128)(2,1)S(1)}, u32[]{:S(2)}, u32[]{:S(2)}) collective-permute-start(bf16[256,256]{1,0:T(8,128)(2,1)S(1)} %get-tuple-element.45), channel_id=1, source_target_pairs={{0,4},{1,5},{2,6},{3,7},{4,0},{5,1},{6,2},{7,3},{8,12},{9,13},{10,... | collective-permute-start | bytes 393224 | tf_op jit(solution)/shard_map/ppermute | solution.py:327
  33.5 10.5 %collective-permute-start.16 = (bf16[256,256]{1,0:T(8,128)(2,1)S(1)}, bf16[256,256]{1,0:T(8,128)(2,1)S(1)}, u32[]{:S(2)}, u32[]{:S(2)}) collective-permute-start(bf16[256,256]{1,0:T(8,128)(2,1)S(1)} %get-tuple-element.57), channel_id=1, source_target_pairs={{0,2},{1,3},{2,0},{3,1},{4,6},{5,7},{6,4},{7,5},{8,10},{9,11},{10,... | collective-permute-start | bytes 393224 | tf_op jit(solution)/shard_map/ppermute | solution.py:327
  36.6 9.3 %collective-permute-start.17 = (bf16[256,256]{1,0:T(8,128)(2,1)S(1)}, bf16[256,256]{1,0:T(8,128)(2,1)S(1)}, u32[]{:S(2)}, u32[]{:S(2)}) collective-permute-start(bf16[256,256]{1,0:T(8,128)(2,1)S(1)} %get-tuple-element.58), channel_id=1, source_target_pairs={{0,4},{1,5},{2,6},{3,7},{4,0},{5,1},{6,2},{7,3},{8,12},{9,13},{10,... | collective-permute-start | bytes 393224 | tf_op jit(solution)/shard_map/ppermute | solution.py:327
  42.0 5.9 %collective-permute-start.18 = (bf16[256,256]{1,0:T(8,128)(2,1)S(1)}, bf16[256,256]{1,0:T(8,128)(2,1)S(1)}, u32[]{:S(2)}, u32[]{:S(2)}) collective-permute-start(bf16[256,256]{1,0:T(8,128)(2,1)S(1)} %get-tuple-element.59), channel_id=1, source_target_pairs={{0,6},{1,7},{2,4},{3,5},{4,2},{5,3},{6,0},{7,1},{8,14},{9,15},{10,... | collective-permute-start | bytes 393224 | tf_op jit(solution)/shard_map/ppermute | solution.py:327
  42.2 8.4 %collective-permute-start.22 = (bf16[256,256]{1,0:T(8,128)(2,1)S(1)}, bf16[256,256]{1,0:T(8,128)(2,1)S(1)}, u32[]{:S(2)}, u32[]{:S(2)}) collective-permute-start(bf16[256,256]{1,0:T(8,128)(2,1)S(1)} %fusion.3), channel_id=1, source_target_pairs={{8,0},{16,8},{24,16},{0,24},{9,1},{17,9},{25,17},{1,25},{10,2},{18... | collective-permute-start | bytes 393224 | tf_op jit(solution)/shard_map/ppermute | solution.py:413
  48.0 5.0 %collective-permute-start.21 = (bf16[256,256]{1,0:T(8,128)(2,1)S(1)}, bf16[256,256]{1,0:T(8,128)(2,1)S(1)}, u32[]{:S(2)}, u32[]{:S(2)}) collective-permute-start(bf16[256,256]{1,0:T(8,128)(2,1)S(1)} %fusion.10), channel_id=1, source_target_pairs={{8,0},{16,8},{24,16},{0,24},{9,1},{17,9},{25,17},{1,25},{10,2},{18... | collective-permute-start | bytes 393224 | tf_op jit(solution)/shard_map/ppermute | solution.py:413
  48.1 3.0 %collective-permute-start.15 = (bf16[128,1024]{1,0:T(8,128)(2,1)S(1)}, bf16[128,1024]{1,0:T(8,128)(2,1)S(1)}, u32[]{:S(2)}, u32[]{:S(2)}) collective-permute-start(bf16[128,1024]{1,0:T(8,128)(2,1)S(1)} %get-tuple-element.54), channel_id=1, source_target_pairs={{0,1},{1,0},{2,3},{3,2},{4,5},{5,4},{6,7},{7,6},{8,9},{9,8},{10,11... | collective-permute-start | bytes 786440 | tf_op jit(solution)/shard_map/ppermute | solution.py:327
  49.9 1.7 %collective-permute-start.19 = (bf16[128,1024]{1,0:T(8,128)(2,1)S(1)}, bf16[128,1024]{1,0:T(8,128)(2,1)S(1)}, u32[]{:S(2)}, u32[]{:S(2)}) collective-permute-start(bf16[128,1024]{1,0:T(8,128)(2,1)S(1)} %get-tuple-element.63), channel_id=1, source_target_pairs={{0,1},{1,0},{2,3},{3,2},{4,5},{5,4},{6,7},{7,6},{8,9},{9,8},{10,11... | collective-permute-start | bytes 786440 | tf_op jit(solution)/shard_map/ppermute | solution.py:327
  50.5 2.5 %collective-permute-start.20 = (f32[2,128,256]{2,1,0:T(8,128)S(1)}, f32[2,128,256]{2,1,0:T(8,128)S(1)}, u32[]{:S(2)}, u32[]{:S(2)}) collective-permute-start(f32[2,128,256]{2,1,0:T(8,128)S(1)} %pad_maximum_fusion.1), channel_id=1, source_target_pairs={{0,1},{1,0},{2,3},{3,2},{4,5},{5,4},{6,7},{7,6},{8,9},{9,8},{10,11... | collective-permute-start | bytes 786440 | tf_op jit(solution)/shard_map/ppermute | solution.py:327
  50.6 2.5 %collective-permute-start.23 = (bf16[256,256]{1,0:T(8,128)(2,1)S(1)}, bf16[256,256]{1,0:T(8,128)(2,1)S(1)}, u32[]{:S(2)}, u32[]{:S(2)}) collective-permute-start(bf16[256,256]{1,0:T(8,128)(2,1)S(1)} %collective-permute-done.22.refs_2_), channel_id=1, source_target_pairs={{0,1},{1,0},{2,3},{3,2},{4,5},{5,4},{6,7},{7,6},{8,9},{9,8},{10,11... | collective-permute-start | bytes 393224 | tf_op jit(solution)/shard_map/ppermute | solution.py:327
  (4 other events, 57.9 us)
where the time goes:
time: 56.1 us; the launch traced here: 55.7 us
  starting transfers between devices  31.2 us (56%)
  waiting for transfers between devices  11.3 us (20%)
  Pallas kernels  9.75 us (17%)
  other arithmetic  1.75 us (3%)
  local copies, waits for them, and re-layouts  0.9 us (2%)
  between operations  0.84 us (1%)
    ppermute x21, starting transfers between devices, swap(): return lax.ppermute(value, 'seq', [(i, i ^ k) for i in range(seq_count)])  26.7 us
    pallas_call x6, Pallas kernels, call(): pl.pallas_call(kernel, out_shape=out_shape, in_specs=[smem] * len(scalars...  9.75 us
    ppermute x21, waiting for transfers between devices, swap(): return lax.ppermute(value, 'seq', [(i, i ^ k) for i in range(seq_count)])  6.34 us
    ppermute x2, waiting for transfers between devices, local(): lax.ppermute(o, 'dp', [(i, (i + 1) % dp_count) for i in range(dp_count)])  4.63 us
    ppermute x2, starting transfers between devices, local(): lax.ppermute(o, 'dp', [(i, (i + 1) % dp_count) for i in range(dp_count)])  4.39 us
  transfers between devices with their start and end apart: 25, of which 8 were waited for; matrix products, arithmetic and copies ran while one was open for 5% of the time, Pallas kernels for 15%

commit v1 on v0

--- a/solution.py
+++ b/solution.py
@@ -210,13 +210,8 @@
         dkv_s[back - 1, key_rows_, K_COLS] = (dk * INV_ROOT).astype(jnp.bfloat16)
         dkv_s[back - 1, key_rows_, V_COLS] = dv.astype(jnp.bfloat16)
 
-    def one_side(back):
-        grad_block(back, whole, one)
-        unused = pl.ds(pl.multiple_of((1 - core) * half_cols, half_cols), half_cols)
-        ds_out[back - 1, :, unused] = jnp.zeros((keys, half_cols), jnp.bfloat16)
-
     each(1, both_end, lambda back: grad_block(back, whole, both))
-    each(later_count, count, one_side)
+    each(later_count, count, lambda back: grad_block(back, whole, one))
 
     @pl.when(trim)
     def _():
@@ -234,8 +229,8 @@
     own_out, dq_mine, dq_theirs, dq_s = refs[-4:]
     keys = kv_ref.shape[1]
     tok = keys // 2
-    _, chip, _, _, lows = place(info_ref, doc_ref, tok, pairs)
-    count = blocks_back(chip, lows[0], keys)
+    core, chip, _, _, lows = place(info_ref, doc_ref, tok, pairs)
+    count, later_count = (blocks_back(chip, low, keys) for low in lows)
     k_tile = kv_ref[0, :, K_COLS]
     dk = jnp.zeros((keys, HD), jnp.float32)
     dv = jnp.zeros((keys, HD), jnp.float32)
@@ -255,7 +250,15 @@
             dq_s[:, cols] += dot(k_tile, ds_ref[back - 1, :, cols], TN)
         return carry
 
-    lax.fori_loop(1, count, query_step, 0)
+    def one_side_step(back, carry):
+        k_tile = kv_ref[back, :, K_COLS]
+        for at in range(0, PER_KV * tok, keys):
+            cols = pl.ds(pl.multiple_of(core * PER_KV * tok + at, keys), keys)
+            dq_s[:, cols] += dot(k_tile, ds_ref[back - 1, :, cols], TN)
+        return carry
+
+    lax.fori_loop(1, later_count, query_step, 0)
+    lax.fori_loop(later_count, count, one_side_step, 0)
     for half, dq_ref in enumerate((dq_mine, dq_theirs)):
         for h in range(PER_KV):
             block = dq_s[:, pl.ds((half * PER_KV + h) * tok, tok)] * INV_ROOT

time: 56.1 us -> 56.6 us (level)
  starting transfers between devices: 31.2 us -> 35 us
  waiting for transfers between devices: 11.3 us -> 7.53 us
    ppermute x2, starting transfers between devices: 0.12 us -> 10.2 us  [local(): lax.ppermute(prev_sum, 'dp', [((i + 1) % dp_count, i) for i in range(dp_c...]
    ppermute x21, starting transfers between devices: 26.7 us -> 20.4 us  [swap(): return lax.ppermute(value, 'seq', [(i, i ^ k) for i in range(seq_count)])]
    ppermute x21, waiting for transfers between devices: 6.34 us -> 2.9 us  [swap(): return lax.ppermute(value, 'seq', [(i, i ^ k) for i in range(seq_count)])]
  transfers between devices with their start and end apart: 25 -> 25, of which waited for: 8 -> 6; matrix products, arithmetic and copies ran while one was open for 5% -> 5% of each run, Pallas kernels for 15% -> 15%
where the time goes in v1:
time: 56.6 us; the launch traced here: 55.7 us
  starting transfers between devices  35 us (62%)
  Pallas kernels  9.74 us (17%)
  waiting for transfers between devices  7.53 us (13%)
  other arithmetic  1.75 us (3%)
  local copies, waits for them, and re-layouts  0.9 us (2%)
  between operations  0.83 us (1%)
    ppermute x21, starting transfers between devices, swap(): return lax.ppermute(value, 'seq', [(i, i ^ k) for i in range(seq_count)])  20.4 us
    ppermute x2, starting transfers between devices, local(): lax.ppermute(prev_sum, 'dp', [((i + 1) % dp_count, i) for i in range(dp_c...  10.2 us
    pallas_call x6, Pallas kernels, call(): pl.pallas_call(kernel, out_shape=out_shape, in_specs=[smem] * len(scalars...  9.74 us
    ppermute x2, waiting for transfers between devices, local(): lax.ppermute(o, 'dp', [(i, (i + 1) % dp_count) for i in range(dp_count)])  4.63 us
    ppermute x2, starting transfers between devices, local(): lax.ppermute(o, 'dp', [(i, (i + 1) % dp_count) for i in range(dp_count)])  4.39 us
    ppermute x21, waiting for transfers between devices, swap(): return lax.ppermute(value, 'seq', [(i, i ^ k) for i in range(seq_count)])  2.9 us
  transfers between devices with their start and end apart: 25, of which 6 were waited for; matrix products, arithmetic and copies ran while one was open for 5% of the time, Pallas kernels for 15%

profile of v1, /device:TPU:0, one launch (start us, length us, event | category | flops | bytes accessed | tf_op | source)
XLA Modules:
  0.0 55.7 jit_solution(4875886085646952488)
XLA Ops:
  1.3 0.8 %constant_dynamic-slice_fusion.2 = (bf16[128,128]{1,0:T(8,128)(2,1)S(1)}, bf16[128,128]{1,0:T(8,128)(2,1)S(1)}, bf16[128,128]{1,0:T(8,128)(2,1)S(1)}, bf16[128,128]{1,0:T(8,128)(2,1)S(1)}) fusion(bf16[128,512]{1,0:T(8,128)(2,1)} %param.7, s32[]{:T(128)S(6)} %select_n.123, s32[]{:T(128)S(6)} %select_n.122, bf16[128,512]{1,0:T(8,128)(2,1)} %param.6), kind=kLoop, calls=%fused_computation.44 | loop fusion | bytes 262152 | tf_op jit(solution)/shard_map/dynamic_slice | solution.py:338
  3.4 2.8 %collective-permute-start.4 = (bf16[256,256]{1,0:T(8,128)(2,1)S(1)}, bf16[256,256]{1,0:T(8,128)(2,1)S(1)}, u32[]{:S(2)}, u32[]{:S(2)}) collective-permute-start(bf16[256,256]{1,0:T(8,128)(2,1)S(1)} %maximum_maximum_fusion.refs_0_), channel_id=1, source_target_pairs={{0,8},{8,16},{16,24},{24,0},{1,9},{9,17},{17,25},{25,1},{2,10},{10... | collective-permute-start | bytes 393224 | tf_op jit(solution)/shard_map/ppermute | solution.py:344
  6.3 1.6 %collective-permute-start.11 = (bf16[256,256]{1,0:T(8,128)(2,1)S(1)}, bf16[256,256]{1,0:T(8,128)(2,1)S(1)}, u32[]{:S(2)}, u32[]{:S(2)}) collective-permute-start(bf16[256,256]{1,0:T(8,128)(2,1)S(1)} %maximum_maximum_fusion.1.refs_1_.refs_0_), channel_id=1, source_target_pairs={{0,8},{8,16},{16,24},{24,0},{1,9},{9,17},{17,25},{25,1},{2,10},{10... | collective-permute-start | bytes 393224 | tf_op jit(solution)/shard_map/ppermute | solution.py:344
  7.8 4.6 %collective-permute-done.4.refs_4_ = bf16[256,256]{1,0:T(8,128)(2,1)S(1)} collective-permute-done((bf16[256,256]{1,0:T(8,128)(2,1)S(1)}, bf16[256,256]{1,0:T(8,128)(2,1)S(1)}, u32[]{:S(2)}, u32[]{:S(2)}) %collective-permute-start.4) | collective-permute-done | bytes 131104 | tf_op jit(solution)/shard_map/ppermute | solution.py:344
  12.5 1.8 %collective-permute-start.5 = (bf16[256,256]{1,0:T(8,128)(2,1)S(1)}, bf16[256,256]{1,0:T(8,128)(2,1)S(1)}, u32[]{:S(2)}, u32[]{:S(2)}) collective-permute-start(bf16[256,256]{1,0:T(8,128)(2,1)S(1)} %get-tuple-element.80), channel_id=1, source_target_pairs={{0,2},{1,3},{2,0},{3,1},{4,6},{5,7},{6,4},{7,5},{8,10},{9,11},{10,... | collective-permute-start | bytes 393224 | tf_op jit(solution)/shard_map/ppermute | solution.py:330
  14.3 1.5 %collective-permute-start.6 = (bf16[256,256]{1,0:T(8,128)(2,1)S(1)}, bf16[256,256]{1,0:T(8,128)(2,1)S(1)}, u32[]{:S(2)}, u32[]{:S(2)}) collective-permute-start(bf16[256,256]{1,0:T(8,128)(2,1)S(1)} %get-tuple-element.79), channel_id=1, source_target_pairs={{0,4},{1,5},{2,6},{3,7},{4,0},{5,1},{6,2},{7,3},{8,12},{9,13},{10,... | collective-permute-start | bytes 393224 | tf_op jit(solution)/shard_map/ppermute | solution.py:330
  15.9 1.6 %collective-permute-start.7 = (bf16[256,256]{1,0:T(8,128)(2,1)S(1)}, bf16[256,256]{1,0:T(8,128)(2,1)S(1)}, u32[]{:S(2)}, u32[]{:S(2)}) collective-permute-start(bf16[256,256]{1,0:T(8,128)(2,1)S(1)} %get-tuple-element.78), channel_id=1, source_target_pairs={{0,6},{1,7},{2,4},{3,5},{4,2},{5,3},{6,0},{7,1},{8,14},{9,15},{10,... | collective-permute-start | bytes 393224 | tf_op jit(solution)/shard_map/ppermute | solution.py:330
  18.1 1.4 %collective-permute-start.13 = (bf16[256,256]{1,0:T(8,128)(2,1)S(1)}, bf16[256,256]{1,0:T(8,128)(2,1)S(1)}, u32[]{:S(2)}, u32[]{:S(2)}) collective-permute-start(bf16[256,256]{1,0:T(8,128)(2,1)S(1)} %get-tuple-element.76), channel_id=1, source_target_pairs={{0,4},{1,5},{2,6},{3,7},{4,0},{5,1},{6,2},{7,3},{8,12},{9,13},{10,... | collective-permute-start | bytes 393224 | tf_op jit(solution)/shard_map/ppermute | solution.py:330
  19.5 3.5 %own.1 = (bf16[2,2,2,1024,128]{4,3,2,1,0:T(8,128)(2,1)S(1)}, f32[2,2,256,2048]{3,2,1,0:T(8,128)S(1)}, f32[2,3,2048]{2,1,0:T(4,128)S(1)}) custom-call(s32[2]{0:T(128)S(1)} %pad_add_fusion.info_ref, s32[16]{0:T(128)S(1)} %copy-done.2, bf16[256,256]{1,0:T(8,128)(2,1)S(1)} %maximum_maximum_fusion.refs_0_, ...), custom_call_target="tpu_custom_call" | custom-call | flops 536870912 | bytes 10797056 | tf_op jit(solution)/shard_map/own/pallas_call | solution.py:298
  23.0 1.6 %collective-permute-start.14 = (bf16[256,256]{1,0:T(8,128)(2,1)S(1)}, bf16[256,256]{1,0:T(8,128)(2,1)S(1)}, u32[]{:S(2)}, u32[]{:S(2)}) collective-permute-start(bf16[256,256]{1,0:T(8,128)(2,1)S(1)} %get-tuple-element.75), channel_id=1, source_target_pairs={{0,6},{1,7},{2,4},{3,5},{4,2},{5,3},{6,0},{7,1},{8,14},{9,15},{10,... | collective-permute-start | bytes 393224 | tf_op jit(solution)/shard_map/ppermute | solution.py:330
  25.4 2.4 %collective-permute-start.10 = (bf16[256,256]{1,0:T(8,128)(2,1)S(1)}, bf16[256,256]{1,0:T(8,128)(2,1)S(1)}, u32[]{:S(2)}, u32[]{:S(2)}) collective-permute-start(bf16[256,256]{1,0:T(8,128)(2,1)S(1)} %get-tuple-element.46), channel_id=1, source_target_pairs={{0,6},{1,7},{2,4},{3,5},{4,2},{5,3},{6,0},{7,1},{8,14},{9,15},{10,... | collective-permute-start | bytes 393224 | tf_op jit(solution)/shard_map/ppermute | solution.py:330
  27.9 1.7 %collective-permute-start.8 = (bf16[256,256]{1,0:T(8,128)(2,1)S(1)}, bf16[256,256]{1,0:T(8,128)(2,1)S(1)}, u32[]{:S(2)}, u32[]{:S(2)}) collective-permute-start(bf16[256,256]{1,0:T(8,128)(2,1)S(1)} %get-tuple-element.44), channel_id=1, source_target_pairs={{0,2},{1,3},{2,0},{3,1},{4,6},{5,7},{6,4},{7,5},{8,10},{9,11},{10,... | collective-permute-start | bytes 393224 | tf_op jit(solution)/shard_map/ppermute | solution.py:330
  29.6 0.7 %collective-permute-done.14.refs_3_ = bf16[256,256]{1,0:T(8,128)(2,1)S(1)} collective-permute-done((bf16[256,256]{1,0:T(8,128)(2,1)S(1)}, bf16[256,256]{1,0:T(8,128)(2,1)S(1)}, u32[]{:S(2)}, u32[]{:S(2)}) %collective-permute-start.14) | collective-permute-done | bytes 131104 | tf_op jit(solution)/shard_map/ppermute | solution.py:330
  30.4 0.9 %reach_1.1 = (bf16[256,256]{1,0:T(8,128)(2,1)S(1)}, bf16[256,256]{1,0:T(8,128)(2,1)S(1)}, bf16[256,256]{1,0:T(8,128)(2,1)S(1)}, bf16[256,256]{1,0:T(8,128)(2,1)S...) custom-call(s32[2]{0:T(128)S(1)} %pad_add_fusion.info_ref, ...), custom_call_target="tpu_custom_call" | custom-call | flops 2147483648 | bytes 8200192 | tf_op jit(solution)/shard_map/reach_1/pallas_call | solution.py:298
  31.3 2.6 %collective-permute-start.16 = (bf16[256,256]{1,0:T(8,128)(2,1)S(1)}, bf16[256,256]{1,0:T(8,128)(2,1)S(1)}, u32[]{:S(2)}, u32[]{:S(2)}) collective-permute-start(bf16[256,256]{1,0:T(8,128)(2,1)S(1)} %get-tuple-element.57), channel_id=1, source_target_pairs={{0,2},{1,3},{2,0},{3,1},{4,6},{5,7},{6,4},{7,5},{8,10},{9,11},{10,... | collective-permute-start | bytes 393224 | tf_op jit(solution)/shard_map/ppermute | solution.py:330
  33.9 1.0 %collective-permute-start.17 = (bf16[256,256]{1,0:T(8,128)(2,1)S(1)}, bf16[256,256]{1,0:T(8,128)(2,1)S(1)}, u32[]{:S(2)}, u32[]{:S(2)}) collective-permute-start(bf16[256,256]{1,0:T(8,128)(2,1)S(1)} %get-tuple-element.58), channel_id=1, source_target_pairs={{0,4},{1,5},{2,6},{3,7},{4,0},{5,1},{6,2},{7,3},{8,12},{9,13},{10,... | collective-permute-start | bytes 393224 | tf_op jit(solution)/shard_map/ppermute | solution.py:330
  34.9 1.4 %collective-permute-start.18 = (bf16[256,256]{1,0:T(8,128)(2,1)S(1)}, bf16[256,256]{1,0:T(8,128)(2,1)S(1)}, u32[]{:S(2)}, u32[]{:S(2)}) collective-permute-start(bf16[256,256]{1,0:T(8,128)(2,1)S(1)} %get-tuple-element.59), channel_id=1, source_target_pairs={{0,6},{1,7},{2,4},{3,5},{4,2},{5,3},{6,0},{7,1},{8,14},{9,15},{10,... | collective-permute-start | bytes 393224 | tf_op jit(solution)/shard_map/ppermute | solution.py:330
  36.4 9.2 %collective-permute-start.22 = (bf16[256,256]{1,0:T(8,128)(2,1)S(1)}, bf16[256,256]{1,0:T(8,128)(2,1)S(1)}, u32[]{:S(2)}, u32[]{:S(2)}) collective-permute-start(bf16[256,256]{1,0:T(8,128)(2,1)S(1)} %fusion.3), channel_id=1, source_target_pairs={{8,0},{16,8},{24,16},{0,24},{9,1},{17,9},{25,17},{1,25},{10,2},{18... | collective-permute-start | bytes 393224 | tf_op jit(solution)/shard_map/ppermute | solution.py:416
  45.5 1.6 %rest_0.1 = (f32[256,256]{1,0:T(8,128)S(1)}, bf16[128,1024]{1,0:T(8,128)(2,1)S(1)}, bf16[128,1024]{1,0:T(8,128)(2,1)S(1)}) custom-call(s32[2]{0:T(128)S(1)} %pad_add_fusion.info_ref, s32[16]{0:T(128)S(1)} %copy-done.2, bf16[2,2,2,1024,128]{4,3,2,1,0:T(8,128)(2,1)S(1)} %get-tuple-element.39.qo_ref, ...), custom_call_target="tpu_custom_call" | custom-call | flops 939524096 | bytes 16195584 | tf_op jit(solution)/shard_map/rest_0/pallas_call | solution.py:298
  47.4 1.1 %collective-permute-start.21 = (bf16[256,256]{1,0:T(8,128)(2,1)S(1)}, bf16[256,256]{1,0:T(8,128)(2,1)S(1)}, u32[]{:S(2)}, u32[]{:S(2)}) collective-permute-start(bf16[256,256]{1,0:T(8,128)(2,1)S(1)} %fusion.10), channel_id=1, source_target_pairs={{8,0},{16,8},{24,16},{0,24},{9,1},{17,9},{25,17},{1,25},{10,2},{18... | collective-permute-start | bytes 393224 | tf_op jit(solution)/shard_map/ppermute | solution.py:416
  48.5 1.6 %rest_1.1 = (f32[256,256]{1,0:T(8,128)S(1)}, bf16[128,1024]{1,0:T(8,128)(2,1)S(1)}, bf16[128,1024]{1,0:T(8,128)(2,1)S(1)}) custom-call(s32[2]{0:T(128)S(1)} %pad_add_fusion.info_ref, s32[16]{0:T(128)S(1)} %copy-done.2, bf16[2,2,2,1024,128]{4,3,2,1,0:T(8,128)(2,1)S(1)} %get-tuple-element.39.qo_ref, ...), custom_call_target="tpu_custom_call" | custom-call | flops 939524096 | bytes 16195584 | tf_op jit(solution)/shard_map/rest_1/pallas_call | solution.py:298
  52.0 1.0 %pad_maximum_fusion = bf16[128,4096]{1,0:T(8,128)(2,1)} fusion(bf16[128,1024]{1,0:T(8,128)(2,1)S(1)} %get-tuple-element.74, bf16[128,1024]{1,0:T(8,128)(2,1)S(1)} %get-tuple-element.72, bf16[128,1024]{1,0:T(8,128)(2,1)S(1)} %get-tuple-element.73, bf16[128,1024]{1,0:T(8,128)(2,1)S(1)} %get-tuple-element.71), kind=kLoop, calls=%fused_computation | loop fusion | flops 4194304 | bytes 2097152 | tf_op jit(solution)/shard_map/concatenate | solution.py:441
  53.5 1.0 %collective-permute-done.24.refs_6_ = bf16[256,256]{1,0:T(8,128)(2,1)S(1)} collective-permute-done((bf16[256,256]{1,0:T(8,128)(2,1)S(1)}, bf16[256,256]{1,0:T(8,128)(2,1)S(1)}, u32[]{:S(2)}, u32[]{:S(2)}) %collective-permute-start.24) | collective-permute-done | bytes 131104 | tf_op jit(solution)/shard_map/ppermute | solution.py:330
  54.4 1.3 %finish.1 = (bf16[128,512]{1,0:T(8,128)(2,1)}, bf16[128,512]{1,0:T(8,128)(2,1)}) custom-call(s32[2]{0:T(128)S(1)} %pad_add_fusion.info_ref, f32[256,256]{1,0:T(8,128)S(1)} %fusion.6.refs_0_, f32[256,256]{1,0:T(8,128)S(1)} %fusion.13.refs_1_, bf16[256,256]{1,0:T(8,128)(2,1)S(1)} %collective-permute-done.22.refs_2_, ...), custom_call_target="tpu_custom_call" | custom-call | bytes 1572864 | tf_op jit(solution)/shard_map/finish/pallas_call | solution.py:298
  (56 shorter events, 6.0 us)
Async XLA Ops:
  0.7 1.7 %collective-permute-start = (bf16[128,512]{1,0:T(8,128)(2,1)}, bf16[128,512]{1,0:T(8,128)(2,1)S(1)}, u32[]{:S(2)}, u32[]{:S(2)}) collective-permute-start(bf16[128,512]{1,0:T(8,128)(2,1)} %param.6), channel_id=1, source_target_pairs={{0,1},{1,0},{2,3},{3,2},{4,5},{5,4},{6,7},{7,6},{8,9},{9,8},{10,11... | collective-permute-start | bytes 393224 | tf_op jit(solution)/shard_map/ppermute | solution.py:330
  1.2 1.6 %collective-permute-start.1 = (bf16[128,512]{1,0:T(8,128)(2,1)}, bf16[128,512]{1,0:T(8,128)(2,1)S(1)}, u32[]{:S(2)}, u32[]{:S(2)}) collective-permute-start(bf16[128,512]{1,0:T(8,128)(2,1)} %param.7), channel_id=1, source_target_pairs={{0,1},{1,0},{2,3},{3,2},{4,5},{5,4},{6,7},{7,6},{8,9},{9,8},{10,11... | collective-permute-start | bytes 393224 | tf_op jit(solution)/shard_map/ppermute | solution.py:330
  2.8 14.7 %collective-permute-start.2 = (bf16[128,4096]{1,0:T(8,128)(2,1)}, bf16[128,4096]{1,0:T(8,128)(2,1)}, u32[]{:S(2)}, u32[]{:S(2)}) collective-permute-start(bf16[128,4096]{1,0:T(8,128)(2,1)} %refs_2_.1), channel_id=1, source_target_pairs={{0,1},{1,0},{2,3},{3,2},{4,5},{5,4},{6,7},{7,6},{8,9},{9,8},{10,11... | collective-permute-start | bytes 3145736 | tf_op jit(solution)/shard_map/ppermute | solution.py:330
  3.0 15.1 %collective-permute-start.3 = (bf16[128,4096]{1,0:T(8,128)(2,1)}, bf16[128,4096]{1,0:T(8,128)(2,1)}, u32[]{:S(2)}, u32[]{:S(2)}) collective-permute-start(bf16[128,4096]{1,0:T(8,128)(2,1)} %refs_3_.1), channel_id=1, source_target_pairs={{0,1},{1,0},{2,3},{3,2},{4,5},{5,4},{6,7},{7,6},{8,9},{9,8},{10,11... | collective-permute-start | bytes 3145736 | tf_op jit(solution)/shard_map/ppermute | solution.py:330
  3.4 9.1 %collective-permute-start.4 = (bf16[256,256]{1,0:T(8,128)(2,1)S(1)}, bf16[256,256]{1,0:T(8,128)(2,1)S(1)}, u32[]{:S(2)}, u32[]{:S(2)}) collective-permute-start(bf16[256,256]{1,0:T(8,128)(2,1)S(1)} %maximum_maximum_fusion.refs_0_), channel_id=1, source_target_pairs={{0,8},{8,16},{16,24},{24,0},{1,9},{9,17},{17,25},{25,1},{2,10},{10... | collective-permute-start | bytes 393224 | tf_op jit(solution)/shard_map/ppermute | solution.py:344
  6.3 9.6 %collective-permute-start.11 = (bf16[256,256]{1,0:T(8,128)(2,1)S(1)}, bf16[256,256]{1,0:T(8,128)(2,1)S(1)}, u32[]{:S(2)}, u32[]{:S(2)}) collective-permute-start(bf16[256,256]{1,0:T(8,128)(2,1)S(1)} %maximum_maximum_fusion.1.refs_1_.refs_0_), channel_id=1, source_target_pairs={{0,8},{8,16},{16,24},{24,0},{1,9},{9,17},{17,25},{25,1},{2,10},{10... | collective-permute-start | bytes 393224 | tf_op jit(solution)/shard_map/ppermute | solution.py:344
  12.5 10.5 %collective-permute-start.5 = (bf16[256,256]{1,0:T(8,128)(2,1)S(1)}, bf16[256,256]{1,0:T(8,128)(2,1)S(1)}, u32[]{:S(2)}, u32[]{:S(2)}) collective-permute-start(bf16[256,256]{1,0:T(8,128)(2,1)S(1)} %get-tuple-element.80), channel_id=1, source_target_pairs={{0,2},{1,3},{2,0},{3,1},{4,6},{5,7},{6,4},{7,5},{8,10},{9,11},{10,... | collective-permute-start | bytes 393224 | tf_op jit(solution)/shard_map/ppermute | solution.py:330
  14.3 10.3 %collective-permute-start.6 = (bf16[256,256]{1,0:T(8,128)(2,1)S(1)}, bf16[256,256]{1,0:T(8,128)(2,1)S(1)}, u32[]{:S(2)}, u32[]{:S(2)}) collective-permute-start(bf16[256,256]{1,0:T(8,128)(2,1)S(1)} %get-tuple-element.79), channel_id=1, source_target_pairs={{0,4},{1,5},{2,6},{3,7},{4,0},{5,1},{6,2},{7,3},{8,12},{9,13},{10,... | collective-permute-start | bytes 393224 | tf_op jit(solution)/shard_map/ppermute | solution.py:330
  15.9 8.8 %collective-permute-start.7 = (bf16[256,256]{1,0:T(8,128)(2,1)S(1)}, bf16[256,256]{1,0:T(8,128)(2,1)S(1)}, u32[]{:S(2)}, u32[]{:S(2)}) collective-permute-start(bf16[256,256]{1,0:T(8,128)(2,1)S(1)} %get-tuple-element.78), channel_id=1, source_target_pairs={{0,6},{1,7},{2,4},{3,5},{4,2},{5,3},{6,0},{7,1},{8,14},{9,15},{10,... | collective-permute-start | bytes 393224 | tf_op jit(solution)/shard_map/ppermute | solution.py:330
  17.5 12.1 %collective-permute-start.12 = (bf16[256,256]{1,0:T(8,128)(2,1)S(1)}, bf16[256,256]{1,0:T(8,128)(2,1)S(1)}, u32[]{:S(2)}, u32[]{:S(2)}) collective-permute-start(bf16[256,256]{1,0:T(8,128)(2,1)S(1)} %get-tuple-element.77), channel_id=1, source_target_pairs={{0,2},{1,3},{2,0},{3,1},{4,6},{5,7},{6,4},{7,5},{8,10},{9,11},{10,... | collective-permute-start | bytes 393224 | tf_op jit(solution)/shard_map/ppermute | solution.py:330
  18.1 11.5 %collective-permute-start.13 = (bf16[256,256]{1,0:T(8,128)(2,1)S(1)}, bf16[256,256]{1,0:T(8,128)(2,1)S(1)}, u32[]{:S(2)}, u32[]{:S(2)}) collective-permute-start(bf16[256,256]{1,0:T(8,128)(2,1)S(1)} %get-tuple-element.76), channel_id=1, source_target_pairs={{0,4},{1,5},{2,6},{3,7},{4,0},{5,1},{6,2},{7,3},{8,12},{9,13},{10,... | collective-permute-start | bytes 393224 | tf_op jit(solution)/shard_map/ppermute | solution.py:330
  23.0 7.3 %collective-permute-start.14 = (bf16[256,256]{1,0:T(8,128)(2,1)S(1)}, bf16[256,256]{1,0:T(8,128)(2,1)S(1)}, u32[]{:S(2)}, u32[]{:S(2)}) collective-permute-start(bf16[256,256]{1,0:T(8,128)(2,1)S(1)} %get-tuple-element.75), channel_id=1, source_target_pairs={{0,6},{1,7},{2,4},{3,5},{4,2},{5,3},{6,0},{7,1},{8,14},{9,15},{10,... | collective-permute-start | bytes 393224 | tf_op jit(solution)/shard_map/ppermute | solution.py:330
  25.4 9.4 %collective-permute-start.10 = (bf16[256,256]{1,0:T(8,128)(2,1)S(1)}, bf16[256,256]{1,0:T(8,128)(2,1)S(1)}, u32[]{:S(2)}, u32[]{:S(2)}) collective-permute-start(bf16[256,256]{1,0:T(8,128)(2,1)S(1)} %get-tuple-element.46), channel_id=1, source_target_pairs={{0,6},{1,7},{2,4},{3,5},{4,2},{5,3},{6,0},{7,1},{8,14},{9,15},{10,... | collective-permute-start | bytes 393224 | tf_op jit(solution)/shard_map/ppermute | solution.py:330
  27.9 8.4 %collective-permute-start.8 = (bf16[256,256]{1,0:T(8,128)(2,1)S(1)}, bf16[256,256]{1,0:T(8,128)(2,1)S(1)}, u32[]{:S(2)}, u32[]{:S(2)}) collective-permute-start(bf16[256,256]{1,0:T(8,128)(2,1)S(1)} %get-tuple-element.44), channel_id=1, source_target_pairs={{0,2},{1,3},{2,0},{3,1},{4,6},{5,7},{6,4},{7,5},{8,10},{9,11},{10,... | collective-permute-start | bytes 393224 | tf_op jit(solution)/shard_map/ppermute | solution.py:330
  29.6 6.6 %collective-permute-start.9 = (bf16[256,256]{1,0:T(8,128)(2,1)S(1)}, bf16[256,256]{1,0:T(8,128)(2,1)S(1)}, u32[]{:S(2)}, u32[]{:S(2)}) collective-permute-start(bf16[256,256]{1,0:T(8,128)(2,1)S(1)} %get-tuple-element.45), channel_id=1, source_target_pairs={{0,4},{1,5},{2,6},{3,7},{4,0},{5,1},{6,2},{7,3},{8,12},{9,13},{10,... | collective-permute-start | bytes 393224 | tf_op jit(solution)/shard_map/ppermute | solution.py:330
  31.3 16.0 %collective-permute-start.16 = (bf16[256,256]{1,0:T(8,128)(2,1)S(1)}, bf16[256,256]{1,0:T(8,128)(2,1)S(1)}, u32[]{:S(2)}, u32[]{:S(2)}) collective-permute-start(bf16[256,256]{1,0:T(8,128)(2,1)S(1)} %get-tuple-element.57), channel_id=1, source_target_pairs={{0,2},{1,3},{2,0},{3,1},{4,6},{5,7},{6,4},{7,5},{8,10},{9,11},{10,... | collective-permute-start | bytes 393224 | tf_op jit(solution)/shard_map/ppermute | solution.py:330
  33.9 13.4 %collective-permute-start.17 = (bf16[256,256]{1,0:T(8,128)(2,1)S(1)}, bf16[256,256]{1,0:T(8,128)(2,1)S(1)}, u32[]{:S(2)}, u32[]{:S(2)}) collective-permute-start(bf16[256,256]{1,0:T(8,128)(2,1)S(1)} %get-tuple-element.58), channel_id=1, source_target_pairs={{0,4},{1,5},{2,6},{3,7},{4,0},{5,1},{6,2},{7,3},{8,12},{9,13},{10,... | collective-permute-start | bytes 393224 | tf_op jit(solution)/shard_map/ppermute | solution.py:330
  34.9 12.4 %collective-permute-start.18 = (bf16[256,256]{1,0:T(8,128)(2,1)S(1)}, bf16[256,256]{1,0:T(8,128)(2,1)S(1)}, u32[]{:S(2)}, u32[]{:S(2)}) collective-permute-start(bf16[256,256]{1,0:T(8,128)(2,1)S(1)} %get-tuple-element.59), channel_id=1, source_target_pairs={{0,6},{1,7},{2,4},{3,5},{4,2},{5,3},{6,0},{7,1},{8,14},{9,15},{10,... | collective-permute-start | bytes 393224 | tf_op jit(solution)/shard_map/ppermute | solution.py:330
  36.4 14.5 %collective-permute-start.22 = (bf16[256,256]{1,0:T(8,128)(2,1)S(1)}, bf16[256,256]{1,0:T(8,128)(2,1)S(1)}, u32[]{:S(2)}, u32[]{:S(2)}) collective-permute-start(bf16[256,256]{1,0:T(8,128)(2,1)S(1)} %fusion.3), channel_id=1, source_target_pairs={{8,0},{16,8},{24,16},{0,24},{9,1},{17,9},{25,17},{1,25},{10,2},{18... | collective-permute-start | bytes 393224 | tf_op jit(solution)/shard_map/ppermute | solution.py:416
  47.4 5.7 %collective-permute-start.21 = (bf16[256,256]{1,0:T(8,128)(2,1)S(1)}, bf16[256,256]{1,0:T(8,128)(2,1)S(1)}, u32[]{:S(2)}, u32[]{:S(2)}) collective-permute-start(bf16[256,256]{1,0:T(8,128)(2,1)S(1)} %fusion.10), channel_id=1, source_target_pairs={{8,0},{16,8},{24,16},{0,24},{9,1},{17,9},{25,17},{1,25},{10,2},{18... | collective-permute-start | bytes 393224 | tf_op jit(solution)/shard_map/ppermute | solution.py:416
  48.5 2.9 %collective-permute-start.15 = (bf16[128,1024]{1,0:T(8,128)(2,1)S(1)}, bf16[128,1024]{1,0:T(8,128)(2,1)S(1)}, u32[]{:S(2)}, u32[]{:S(2)}) collective-permute-start(bf16[128,1024]{1,0:T(8,128)(2,1)S(1)} %get-tuple-element.54), channel_id=1, source_target_pairs={{0,1},{1,0},{2,3},{3,2},{4,5},{5,4},{6,7},{7,6},{8,9},{9,8},{10,11... | collective-permute-start | bytes 786440 | tf_op jit(solution)/shard_map/ppermute | solution.py:330
  50.2 1.7 %collective-permute-start.19 = (bf16[128,1024]{1,0:T(8,128)(2,1)S(1)}, bf16[128,1024]{1,0:T(8,128)(2,1)S(1)}, u32[]{:S(2)}, u32[]{:S(2)}) collective-permute-start(bf16[128,1024]{1,0:T(8,128)(2,1)S(1)} %get-tuple-element.63), channel_id=1, source_target_pairs={{0,1},{1,0},{2,3},{3,2},{4,5},{5,4},{6,7},{7,6},{8,9},{9,8},{10,11... | collective-permute-start | bytes 786440 | tf_op jit(solution)/shard_map/ppermute | solution.py:330
  50.8 2.3 %collective-permute-start.20 = (f32[2,128,256]{2,1,0:T(8,128)S(1)}, f32[2,128,256]{2,1,0:T(8,128)S(1)}, u32[]{:S(2)}, u32[]{:S(2)}) collective-permute-start(f32[2,128,256]{2,1,0:T(8,128)S(1)} %pad_maximum_fusion.1), channel_id=1, source_target_pairs={{0,1},{1,0},{2,3},{3,2},{4,5},{5,4},{6,7},{7,6},{8,9},{9,8},{10,11... | collective-permute-start | bytes 786440 | tf_op jit(solution)/shard_map/ppermute | solution.py:330
  50.9 2.5 %collective-permute-start.23 = (bf16[256,256]{1,0:T(8,128)(2,1)S(1)}, bf16[256,256]{1,0:T(8,128)(2,1)S(1)}, u32[]{:S(2)}, u32[]{:S(2)}) collective-permute-start(bf16[256,256]{1,0:T(8,128)(2,1)S(1)} %collective-permute-done.22.refs_2_), channel_id=1, source_target_pairs={{0,1},{1,0},{2,3},{3,2},{4,5},{5,4},{6,7},{7,6},{8,9},{9,8},{10,11... | collective-permute-start | bytes 393224 | tf_op jit(solution)/shard_map/ppermute | solution.py:330
  (4 other events, 57.9 us)
